TPU v7x, 512 devices: a whole 4x8x8 slice. The times are simulated.
512 devices in a mesh: gx: 32 (over y, x), gy: 16 (over z, core).
Axes of the slice: x: 4, y: 8, z: 8, core: 2. Of those that a mesh axis runs over, the one named last changes fastest.
Arguments:
- flow_state: float32 [5, 256, 16384], P(None, 'gx', 'gy'), as said below
- x_codes: int32 [2, 512], P(None, 'gy'), may hold values from 0 to 1
- y_codes: int32 [2, 256], P(None, 'gx'), may hold values from 0 to 1
Outputs:
- increment: float32 [5, 256, 16384], P(None, 'gx', 'gy')
Inputs may be any that keep to these rules, and one draw needn't show every extreme that they name: `flow_state`: density lies in [0.75, 1.33], each velocity in [-0.5, 0.5], pressure in [0.6, 1.4]. `x_codes`: 0: the increment beyond the face is zero; 1: it equals that of the boundary cell. `y_codes`: 0: the increment beyond the face is zero; 1: it equals that of the boundary cell.
All inputs are finite; a program needn't handle non-finite values.
Results may differ from a plain program's by a relative error of at most 0.0003.
Values sent between devices are 32-bit elements; how exact they have to be, the bound alone decides.
A program may use at most 64 MiB of HBM per device.

v0:
```python
import functools

import jax
import jax.numpy as jnp
from jax import lax
from jax.experimental import pallas as pl
from jax.experimental.pallas import tpu as pltpu
from jax.sharding import PartitionSpec as P

NZ = 32
SX = 32
SY = 16
TY = 8
MAIN = 801.0
GROUPS = ((0, (0,)), (2, (4,)), (1, (1, 2)), (1, (3,)))
MESH = pl.DeviceIdType.MESH


def roll(value, shift, axis):
    axis = axis % value.ndim
    return pltpu.roll(value, shift % value.shape[axis], axis)


def lane_of(shape):
    return lax.broadcasted_iota(jnp.int32, shape, len(shape) - 1)


def row_of(shape):
    return lax.broadcasted_iota(jnp.int32, shape, len(shape) - 2)


def five(value):
    return jnp.concatenate([value[0:1], value[1:2], value[1:2], value[1:2], value[2:3]])


def primitives(q):
    inv = 1.0 / q[0]
    u, v, w = q[1] * inv, q[2] * inv, q[3] * inv
    p = 0.4 * (q[4] - 0.5 * (q[1] * u + q[2] * v + q[3] * w))
    c2 = 1.4 * p * inv
    return inv, u, v, w, p, c2, c2 * lax.rsqrt(c2)


def up_y(value):
    here, after = value[..., 1:9, :, :], value[..., 2:10, :, :]
    return roll(jnp.where(lane_of(here.shape) < 32, after, here), -32, -1)


def down_y(value):
    before, here = value[..., 0:8, :, :], value[..., 1:9, :, :]
    return roll(jnp.where(lane_of(here.shape) >= 96, before, here), 32, -1)


def z_difference(value):
    z = lane_of(value.shape) & 31
    after = jnp.where(z == 31, roll(value, 31, -1), roll(value, -1, -1))
    before = jnp.where(z == 0, roll(value, -31, -1), roll(value, 1, -1))
    return after - before


def yz_part(q):
    inv, u, v, w, p, c2, c = primitives(q)
    flux = jnp.stack([q[2], q[1] * v, q[2] * v + p, q[3] * v, v * (q[4] + p)])
    smooth = 400.0 * q
    flux = 0.25 * flux
    inner, wi, pi = q[:, 1:9], w[1:9], p[1:9]
    flux_z = jnp.stack(
        [inner[3], inner[1] * wi, inner[2] * wi, inner[3] * wi + pi, wi * (inner[4] + pi)]
    )
    part = up_y(smooth - flux) + down_y(smooth + flux) - 1600.0 * inner
    part = part - 0.25 * z_difference(flux_z)
    speeds = jnp.stack([v, c])
    return part, jnp.concatenate([down_y(speeds), up_y(speeds)])


def x_part(q, prim):
    inv, u, v, w, p, c2, c = prim
    flux = jnp.stack([q[1], q[1] * u + p, q[2] * u, q[3] * u, u * (q[4] + p)])
    smooth = 400.0 * q
    flux = 0.25 * flux
    return (smooth - flux)[:, 2:10] + (smooth + flux)[:, 0:8]


def x_right(res, prim):
    inv, u, v, w, p, c2, c = prim
    kinetic = 0.5 * (u * u + v * v + w * w)
    dp = 0.4 * (res[4] - u * res[1] - v * res[2] - w * res[3] + kinetic * res[0])
    normal = c * (res[1] - u * res[0])
    return jnp.stack(
        [
            dp - normal,
            c2 * res[0] - dp,
            (res[2] - v * res[0]) * inv,
            (res[3] - w * res[0]) * inv,
            dp + normal,
        ]
    )


def eliminate(lower, upper, main_first, main_last):
    n = len(lower)
    m = [1.0 / main_first]
    g = [upper[0] * m[0]]
    p = [-lower[0] * m[0]]
    for k in range(1, n - 1):
        m.append(1.0 / (MAIN - lower[k] * g[k - 1]))
        g.append(upper[k] * m[k])
        p.append(-(lower[k] * p[k - 1]) * m[k])
    q = [None] * (n - 1)
    q[n - 2] = -g[n - 2]
    for k in range(n - 3, -1, -1):
        p[k] = p[k] - g[k] * p[k + 1]
        q[k] = -(g[k] * q[k + 1])
    last = 1.0 / (main_last + lower[n - 1] * q[n - 2])
    m.append(last)
    own = (-(lower[n - 1] * p[n - 2]) * last, -upper[n - 1] * last, p[0], q[0])
    return m, g, p, q, own


def eliminate_right(right, lower, m, g):
    n = len(right)
    d = [right[0] * five(m[0])]
    for k in range(1, n - 1):
        d.append((right[k] - five(lower[k]) * d[k - 1]) * five(m[k]))
    for k in range(n - 3, -1, -1):
        d[k] = d[k] - five(g[k]) * d[k + 1]
    last = (right[n - 1] - five(lower[n - 1]) * d[n - 2]) * five(m[n - 1])
    return d, last


def put_back(d, p, q, before, own):
    cells = [d[k] + five(p[k]) * before + five(q[k]) * own for k in range(len(d))]
    return cells + [own]


def factor(own):
    to_before, to_after, first_before, first_own = own
    rows = to_before.shape[-2]
    den = 1.0 / (1.0 - to_after * roll(first_before, -1, -2))
    a = to_before * den
    c = to_after * roll(first_own, -1, -2) * den
    return den, to_after * den, a, c


def factor_levels(a, c):
    rows = a.shape[-2]
    levels = []
    step = 1
    while step < rows:
        dn = 1.0 / (1.0 - a * roll(c, step, -2) - c * roll(a, -step, -2))
        an, cn = a * dn, c * dn
        levels.append((dn, an, cn))
        a, c = an * roll(a, step, -2), cn * roll(c, -step, -2)
        step *= 2
    return levels


def reduce_levels(d, levels):
    step = 1
    for dn, an, cn in levels:
        d = dn * d + an * roll(d, step, -2) + cn * roll(d, -step, -2)
        step *= 2
    return d


def y_right(s, rc, half_rc_inv):
    dp = 0.5 * (s[0] + s[4])
    normal = rc * s[2]
    return jnp.stack([dp - normal, s[1], (s[4] - s[0]) * half_rc_inv, s[3], dp + normal])


def swap_groups(value):
    lead = value.shape[:-3]
    half = value.reshape(*lead, 2, 2, 2, 8, 128)
    a, b = half[..., 0, :, :, :], half[..., 1, :, :, :]
    low = (lane_of(a.shape) & 64) == 0
    a, b = jnp.where(low, a, roll(b, 64, -1)), jnp.where(low, roll(a, 64, -1), b)
    half = jnp.stack([a, b], axis=len(lead) + 1)
    a, b = half[..., 0, :, :], half[..., 1, :, :]
    low = (lane_of(a.shape) & 32) == 0
    a, b = jnp.where(low, a, roll(b, 32, -1)), jnp.where(low, roll(a, -32, -1), b)
    half = jnp.stack([a, b], axis=len(lead) + 2)
    return half.reshape(*lead, 8, 8, 128)


def y_bands(speeds):
    vm, cm, vp, cp = (speeds[i].reshape(2, 4, 8, 128) for i in range(4))
    low = jnp.stack([vm - cm, vm, vm + cm])
    high = jnp.stack([vp - cp, vp, vp + cp])
    lower = [-0.25 * low[:, :, k] - 400.0 for k in range(4)]
    upper = [0.25 * high[:, :, k] - 400.0 for k in range(4)]
    return lower, upper


def y_join(own):
    row = row_of(own[0].shape)
    den, high, a, c = factor(own)
    p = jnp.where(row == 0, a, 0.0)
    q = jnp.where(row == 7, 1.0, 0.0)
    a = jnp.where((row == 0) | (row == 7), 0.0, a)
    c = jnp.where(row == 7, 0.0, c)
    levels = factor_levels(a, c)
    p = reduce_levels(p, levels)
    q = reduce_levels(q, levels)
    last = 1.0 / (1.0 - own[0] * roll(q, 1, -2))
    joined = (
        own[0] * roll(p, 1, -2) * last,
        own[1] * last,
        own[2] + own[3] * p,
        own[3] * q,
    )
    return den, high, levels, p, q, last, joined


def y_join_right(d0, last_right, own, den, high, levels, last):
    row = row_of(last_right.shape)
    d = five(den) * last_right + five(high) * roll(d0, -1, -2)
    d = jnp.where(row == 7, 0.0, d)
    d = reduce_levels(d, [tuple(five(part) for part in level) for level in levels])
    joined_last = (last_right + five(own[0]) * roll(d, 1, -2)) * five(last)
    joined_first = d0 + five(own[3]) * d
    return d, joined_last, joined_first


def increments(s, prim, r, half_rc_inv, c2_inv):
    inv, u, v, w, p, c2, c = prim
    dp = 0.5 * (s[0] + s[4])
    dv = (s[4] - s[0]) * half_rc_inv
    dr = (s[1] + dp) * c2_inv
    du, dw = s[2], s[3]
    kinetic = 0.5 * (u * u + v * v + w * w)
    return (
        dr,
        u * dr + r * du,
        v * dr + r * dv,
        w * dr + r * dw,
        kinetic * dr + r * (u * du + v * dv + w * dw) + 2.5 * dp,
    )


def x_code_mask(codes, side):
    ones = (codes[side : side + 1] == 1).astype(jnp.float32)
    spread = jnp.where((lane_of((8, 32)) >> 2) == row_of((8, 32)), ones, 0.0)
    place = jnp.where((row_of((32, 128)) & 3) == (lane_of((32, 128)) >> 5), 1.0, 0.0)
    return jnp.dot(spread, place, preferred_element_type=jnp.float32) > 0.5


def y_code_mask(codes, side):
    ones = jnp.broadcast_to((codes[side : side + 1] == 1).astype(jnp.float32), (8, 8))
    halves = []
    for h in range(2):
        place = jnp.where(row_of((8, 128)) == 4 * h + (lane_of((8, 128)) >> 5), 1.0, 0.0)
        halves.append(jnp.dot(ones, place, preferred_element_type=jnp.float32))
    return jnp.stack(halves) > 0.5


def x_bands(u, c, codes, start, end):
    lam = jnp.stack([u - c, u, u + c])
    lower = [-0.25 * lam[:, k] - 400.0 for k in range(8)]
    upper = [0.25 * lam[:, k + 2] - 400.0 for k in range(8)]
    first = MAIN + jnp.where(x_code_mask(codes, 0)[None] & start, lower[0], 0.0)
    last = MAIN + jnp.where(x_code_mask(codes, 1)[None] & end, upper[7], 0.0)
    lower[0] = jnp.where(start, 0.0, lower[0])
    upper[7] = jnp.where(end, 0.0, upper[7])
    return lower, upper, first, last


def y_ends(lower, upper, codes, start, end):
    row = row_of(lower[0].shape)
    at_start = (row == 0) & start
    at_end = (row == 7) & end
    first = MAIN + jnp.where(at_start & y_code_mask(codes, 0)[None], lower[0], 0.0)
    last = MAIN + jnp.where(at_end & y_code_mask(codes, 1)[None], upper[3], 0.0)
    lower, upper = list(lower), list(upper)
    lower[0] = jnp.where(at_start, 0.0, lower[0])
    upper[3] = jnp.where(at_end, 0.0, upper[3])
    return lower, upper, first, last


def wait_all(ref, sem):
    pltpu.make_async_copy(ref, ref, sem).wait()


def kernel(
    flow,
    x_codes,
    y_codes,
    out,
    q_sc,
    part_sc,
    out_sc,
    speed_sc,
    x_send,
    x_low,
    x_high,
    y_low,
    y_high,
    xm_out,
    xr_out,
    xm_in,
    xr_in,
    xs_out,
    xs_in,
    ym_out,
    yr_out,
    ym_in,
    yr_in,
    ys_out,
    ys_in,
    y_levels,
    in_sem,
    out_sem,
    halo_send,
    halo_recv,
    send_sem,
    recv_sem,
):
    gx, gy = lax.axis_index("gx"), lax.axis_index("gy")
    start_x, end_x = gx == 0, gx == SX - 1
    start_y, end_y = gy == 0, gy == SY - 1

    for b in range(8):
        pltpu.make_async_copy(
            flow.at[:, :, pl.ds(128 * b, 128)], q_sc.at[:, pl.ds(8 * b, 8), :], in_sem
        ).start()

    barrier = pltpu.get_barrier_semaphore()

    def greet_x(k, carry):
        pl.semaphore_signal(
            barrier, inc=1, device_id=(lax.rem(gx + k, SX), gy), device_id_type=MESH
        )
        return carry

    def greet_y(k, carry):
        pl.semaphore_signal(
            barrier, inc=1, device_id=(gx, lax.rem(gy + k, SY)), device_id_type=MESH
        )
        return carry

    lax.fori_loop(1, SX, greet_x, 0)
    lax.fori_loop(1, SY, greet_y, 0)
    wait_all(q_sc, in_sem)

    x_send[0] = q_sc[:, pl.ds(7, 8, stride=8), :]
    x_send[1] = q_sc[:, pl.ds(0, 8, stride=8), :]
    pl.semaphore_wait(barrier, SX + SY - 2)

    x_after, x_before = lax.rem(gx + 1, SX), lax.rem(gx + SX - 1, SX)
    y_after, y_before = lax.rem(gy + 1, SY), lax.rem(gy + SY - 1, SY)
    halos = [
        (x_send.at[0], x_low, (x_after, gy)),
        (x_send.at[1], x_high, (x_before, gy)),
        (q_sc.at[:, pl.ds(56, 8), :], y_low, (gx, y_after)),
        (q_sc.at[:, pl.ds(0, 8), :], y_high, (gx, y_before)),
    ]
    copies = []
    for i, (source, target, device) in enumerate(halos):
        copy = pltpu.make_async_remote_copy(
            src_ref=source,
            dst_ref=target,
            send_sem=halo_send.at[i],
            recv_sem=halo_recv.at[i],
            device_id=device,
            device_id_type=MESH,
        )
        copy.start()
        copies.append(copy)

    def send_x(source, target, slot):
        mine = pl.ds(gx * 4, 4)
        pltpu.make_async_copy(source.at[mine], target.at[mine], recv_sem.at[slot]).start()

        def one(k, carry):
            other = lax.rem(gx + k, SX)
            pltpu.make_async_remote_copy(
                src_ref=source.at[pl.ds(other * 4, 4)],
                dst_ref=target.at[mine],
                send_sem=send_sem.at[slot],
                recv_sem=recv_sem.at[slot],
                device_id=(other, gy),
                device_id_type=MESH,
            ).start()
            return carry

        lax.fori_loop(1, SX, one, 0)

    solver_y = lax.rem(gy, 2) == 0
    tile_y = lax.div(gy, 2)

    def send_y(source, target, slot):
        @pl.when(solver_y)
        def _():
            pltpu.make_async_copy(
                source.at[pl.ds(tile_y * 4, 4)], target.at[pl.ds(gy * 4, 4)], recv_sem.at[slot]
            ).start()

        def one(t, carry):
            @pl.when(gy != 2 * t)
            def _():
                pltpu.make_async_remote_copy(
                    src_ref=source.at[pl.ds(t * 4, 4)],
                    dst_ref=target.at[pl.ds(gy * 4, 4)],
                    send_sem=send_sem.at[slot],
                    recv_sem=recv_sem.at[slot],
                    device_id=(gx, 2 * t),
                    device_id_type=MESH,
                ).start()

            return carry

        lax.fori_loop(0, TY, one, 0)

    for copy in copies:
        copy.wait_recv()
    inner = [q_sc[:, pl.ds(k, 8, stride=8), :] for k in range(8)]
    low = jnp.where(start_x, inner[0], x_low[...])
    high = jnp.where(end_x, inner[7], x_high[...])
    q = jnp.stack([low] + inner + [high], axis=1)
    prim_all = primitives(q)

    lower, upper, first, last = x_bands(prim_all[1], prim_all[6], x_codes[...], start_x, end_x)
    xm, xg, xp, xq, x_own = eliminate(lower, upper, first, last)
    for group, (matrix, families) in enumerate(GROUPS):
        for row in range(4):
            xm_out[pl.ds(group * 32 + row, 8, stride=4), :] = x_own[row][matrix]
    send_x(xm_out, xm_in, 0)

    blocks = q_sc[...].reshape(5, 8, 8, 128)
    y_edge_low = jnp.where(start_y, roll(blocks[:, 0], 96, -1), y_low[...])
    y_edge_high = jnp.where(end_y, roll(blocks[:, 7], 32, -1), y_high[...])
    part, speeds = yz_part(
        jnp.concatenate([y_edge_low[:, None], blocks, y_edge_high[:, None]], axis=1)
    )
    part_sc[...] = part.reshape(5, 64, 128)
    speed_sc[...] = speeds.reshape(4, 64, 128)
    prim = tuple(value[1:9] for value in prim_all)
    residual = x_part(q, prim_all) + jnp.stack(
        [part_sc[:, pl.ds(k, 8, stride=8), :] for k in range(8)], axis=1
    )
    right = x_right(residual, prim)
    xd, x_last = eliminate_right([right[:, k] for k in range(8)], lower, xm, xg)
    zero = jnp.zeros((8, 128), jnp.float32)
    for group, (matrix, families) in enumerate(GROUPS):
        for i in range(2):
            at = group * 32 + 2 * i
            some = i < len(families)
            xr_out[pl.ds(at, 8, stride=4), :] = x_last[families[i]] if some else zero
            xr_out[pl.ds(at + 1, 8, stride=4), :] = xd[0][families[i]] if some else zero
    send_x(xr_out, xr_in, 1)

    speeds = jnp.stack([speed_sc[:, pl.ds(k, 8, stride=8), :] for k in range(8)], axis=1)
    y_lower, y_upper = y_bands(swap_groups(speeds))
    y_lower, y_upper, first, last = y_ends(y_lower, y_upper, y_codes[...], start_y, end_y)
    ym, yg, yp, yq, y_own = eliminate(y_lower, y_upper, first, last)
    y_den, y_high_part, y_lev, y_p, y_q, y_joint, joined = y_join(y_own)
    for group, (matrix, families) in enumerate(GROUPS):
        for h in range(2):
            at = (group * 2 + h) * 4
            for row in range(4):
                line = 7 if row < 2 else 0
                ym_out[pl.ds(at + row, 1), :] = joined[row][matrix, h, line : line + 1]
    send_y(ym_out, ym_in, 3)

    wait_all(xm_in, recv_sem.at[0])
    den, high_part, a, c = factor([xm_in[pl.ds(row, SX, stride=4), :] for row in range(4)])
    levels = factor_levels(a, c)
    wait_all(xr_in, recv_sem.at[1])
    for i in range(2):
        own_last = xr_in[pl.ds(2 * i, SX, stride=4), :]
        own_first = xr_in[pl.ds(2 * i + 1, SX, stride=4), :]
        d = den * own_last + high_part * roll(own_first, -1, 0)
        d = reduce_levels(d, levels)
        xs_out[pl.ds(2 * i, SX, stride=4), :] = roll(d, 1, 0)
        xs_out[pl.ds(2 * i + 1, SX, stride=4), :] = d
    send_x(xs_out, xs_in, 2)

    @pl.when(solver_y)
    def _():
        wait_all(ym_in, recv_sem.at[3])
        den, high_part, a, c = factor([ym_in[pl.ds(row, SY, stride=4), :] for row in range(4)])
        y_levels[0], y_levels[1] = den, high_part
        for i, level in enumerate(factor_levels(a, c)):
            for j in range(3):
                y_levels[2 + 3 * i + j] = level[j]

    r = q[0, 1:9]
    rc = r * prim[6]
    half_rc_inv = 0.5 / rc
    c2_inv = 1.0 / prim[5]

    wait_all(xs_in, recv_sem.at[2])

    def x_value(kind):
        rows = []
        for group, i in ((0, 0), (2, 0), (2, 1), (3, 0), (1, 0)):
            rows.append(xs_in[pl.ds(group * 32 + 2 * i + kind, 8, stride=4), :])
        return jnp.stack(rows)

    solved = jnp.stack(put_back(xd, xp, xq, x_value(0), x_value(1)), axis=1)
    right = swap_groups(y_right(solved, rc, half_rc_inv)).reshape(5, 2, 4, 8, 128)
    yd, y_last = eliminate_right([right[:, :, k] for k in range(4)], y_lower, ym, yg)
    y_d, joined_last, joined_first = y_join_right(
        yd[0], y_last, y_own, y_den, y_high_part, y_lev, y_joint
    )
    line_zero = jnp.zeros((1, 128), jnp.float32)
    for group, (matrix, families) in enumerate(GROUPS):
        for h in range(2):
            for i in range(2):
                at = (group * 2 + h) * 4 + 2 * i
                some = i < len(families)
                yr_out[pl.ds(at, 1), :] = joined_last[families[i], h, 7:8] if some else line_zero
                yr_out[pl.ds(at + 1, 1), :] = (
                    joined_first[families[i], h, 0:1] if some else line_zero
                )
    send_y(yr_out, yr_in, 4)

    @pl.when(solver_y)
    def _():
        wait_all(yr_in, recv_sem.at[4])
        levels = [tuple(y_levels[2 + 3 * i + j] for j in range(3)) for i in range(4)]
        for i in range(2):
            own_last = yr_in[pl.ds(2 * i, SY, stride=4), :]
            own_first = yr_in[pl.ds(2 * i + 1, SY, stride=4), :]
            d = y_levels[0] * own_last + y_levels[1] * roll(own_first, -1, 0)
            d = reduce_levels(d, levels)
            ys_out[pl.ds(2 * i, SY, stride=4), :] = roll(d, 1, 0)
            ys_out[pl.ds(2 * i + 1, SY, stride=4), :] = d
        pltpu.make_async_copy(
            ys_out.at[pl.ds(gy * 4, 4)], ys_in.at[pl.ds(tile_y * 4, 4)], recv_sem.at[5]
        ).start()

        def one(k, carry):
            other = lax.rem(gy + k, SY)
            pltpu.make_async_remote_copy(
                src_ref=ys_out.at[pl.ds(other * 4, 4)],
                dst_ref=ys_in.at[pl.ds(tile_y * 4, 4)],
                send_sem=send_sem.at[5],
                recv_sem=recv_sem.at[5],
                device_id=(gx, other),
                device_id_type=MESH,
            ).start()
            return carry

        lax.fori_loop(1, SY, one, 0)

    wait_all(ys_in, recv_sem.at[5])

    def y_value(kind):
        rows = []
        for group, i in ((0, 0), (2, 0), (2, 1), (3, 0), (1, 0)):
            rows.append(
                jnp.stack([ys_in[pl.ds((group * 2 + h) * 4 + 2 * i + kind, 1), :] for h in range(2)])
            )
        return jnp.stack(rows)

    before, own = y_value(0), y_value(1)
    groups = y_d + five(y_p) * before + five(y_q) * own
    previous = jnp.where(row_of(groups.shape) == 0, before, roll(groups, 1, -2))
    solved = jnp.stack(put_back(yd, yp, yq, previous, groups), axis=2)
    solved = swap_groups(solved.reshape(5, 8, 8, 128))
    for field, value in enumerate(increments(solved, prim, r, half_rc_inv, c2_inv)):
        for k in range(8):
            out_sc[field, pl.ds(k, 8, stride=8), :] = value[k]
    for b in range(8):
        pltpu.make_async_copy(
            out_sc.at[:, pl.ds(8 * b, 8), :], out.at[:, :, pl.ds(128 * b, 128)], out_sem
        ).start()

    for copy in copies:
        copy.wait_send()
    for slot in range(3):
        wait_all(xm_out.at[pl.ds(0, 4 * (SX - 1))], send_sem.at[slot])

    @pl.when(solver_y)
    def _():
        for slot in (3, 4):
            wait_all(ym_out.at[pl.ds(0, 4 * (TY - 1))], send_sem.at[slot])
        wait_all(ys_out.at[pl.ds(0, 4 * (SY - 1))], send_sem.at[5])

    @pl.when(jnp.logical_not(solver_y))
    def _():
        for slot in (3, 4):
            wait_all(ym_out, send_sem.at[slot])

    wait_all(out_sc, out_sem)


def local(flow_state, x_codes, y_codes):
    f32 = jnp.float32

    def vmem(*shape):
        return pltpu.VMEM(shape, f32)

    return pl.pallas_call(
        kernel,
        out_shape=jax.ShapeDtypeStruct(flow_state.shape, f32),
        in_specs=[
            pl.BlockSpec(memory_space=pl.ANY),
            pl.BlockSpec(memory_space=pltpu.VMEM),
            pl.BlockSpec(memory_space=pltpu.VMEM),
        ],
        out_specs=pl.BlockSpec(memory_space=pl.ANY),
        scratch_shapes=[
            vmem(5, 64, 128),
            vmem(5, 64, 128),
            vmem(5, 64, 128),
            vmem(4, 64, 128),
            vmem(2, 5, 8, 128),
            vmem(5, 8, 128),
            vmem(5, 8, 128),
            vmem(5, 8, 128),
            vmem(5, 8, 128),
            vmem(4 * SX, 128),
            vmem(4 * SX, 128),
            vmem(4 * SX, 128),
            vmem(4 * SX, 128),
            vmem(4 * SX, 128),
            vmem(4 * SX, 128),
            vmem(4 * TY, 128),
            vmem(4 * TY, 128),
            vmem(4 * SY, 128),
            vmem(4 * SY, 128),
            vmem(4 * SY, 128),
            vmem(4 * TY, 128),
            vmem(14, SY, 128),
            pltpu.SemaphoreType.DMA,
            pltpu.SemaphoreType.DMA,
            pltpu.SemaphoreType.DMA((4,)),
            pltpu.SemaphoreType.DMA((4,)),
            pltpu.SemaphoreType.DMA((6,)),
            pltpu.SemaphoreType.DMA((6,)),
        ],
        compiler_params=pltpu.CompilerParams(
            collective_id=0, has_side_effects=True, vmem_limit_bytes=32 * 1024 * 1024
        ),
        name="step",
    )(flow_state, x_codes, y_codes)


def solution(mesh):
    return jax.shard_map(
        local,
        mesh=mesh,
        in_specs=(P(None, "gx", "gy"), P(None, "gy"), P(None, "gx")),
        out_specs=P(None, "gx", "gy"),
        check_vma=False,
    )
```

profile of v0, /device:TPU:1, one launch (start us, length us, event | category | flops | bytes accessed | tf_op | source)
XLA Modules:
  0.0 46.7 jit_solution(5326074766128504327)
XLA Ops:
  0.0 0.0 copy-start
  0.0 0.9 %copy-done = f32[5,8,1024]{2,1,0:T(8,128)S(1)} copy-done((f32[5,8,1024]{2,1,0:T(8,128)S(1)}, f32[5,8,1024]{2,1,0:T(8,128)}, u32[]{:S(2)}) %copy-start) | copy-done | bytes 163864
  0.9 0.0 copy-start.1
  0.9 0.7 %copy-done.1 = s32[2,32]{1,0:T(2,128)S(1)} copy-done((s32[2,32]{1,0:T(2,128)S(1)}, s32[2,32]{1,0:T(2,128)}, u32[]{:S(2)}) %copy-start.1) | copy-done | bytes 280
  1.6 0.0 copy-start.2
  1.6 0.7 %copy-done.2 = s32[2,8]{1,0:T(2,128)S(1)} copy-done((s32[2,8]{1,0:T(2,128)S(1)}, s32[2,8]{1,0:T(2,128)}, u32[]{:S(2)}) %copy-start.2) | copy-done | bytes 88
  2.3 43.7 %step.1 = f32[5,8,1024]{2,1,0:T(8,128)S(1)} custom-call(f32[5,8,1024]{2,1,0:T(8,128)S(1)} %copy-done, s32[2,32]{1,0:T(2,128)S(1)} %copy-done.1, s32[2,8]{1,0:T(2,128)S(1)} %copy-done.2), custom_call_target="tpu_custom_call" | custom-call | tf_op jit(solution)/shard_map/step/pallas_call | solution.py:595
  46.0 0.7 %copy.5 = f32[5,8,1024]{2,1,0:T(8,128)} copy(f32[5,8,1024]{2,1,0:T(8,128)S(1)} %step.1) | data formatting | bytes 327680
Async XLA Ops:
  0.0 0.9 %copy-start = (f32[5,8,1024]{2,1,0:T(8,128)S(1)}, f32[5,8,1024]{2,1,0:T(8,128)}, u32[]{:S(2)}) copy-start(f32[5,8,1024]{2,1,0:T(8,128)} %flow.1) | copy-start | bytes 491524
  0.9 0.7 %copy-start.1 = (s32[2,32]{1,0:T(2,128)S(1)}, s32[2,32]{1,0:T(2,128)}, u32[]{:S(2)}) copy-start(s32[2,32]{1,0:T(2,128)} %x_codes.1) | copy-start | bytes 772
  1.6 0.7 %copy-start.2 = (s32[2,8]{1,0:T(2,128)S(1)}, s32[2,8]{1,0:T(2,128)}, u32[]{:S(2)}) copy-start(s32[2,8]{1,0:T(2,128)} %y_codes.1) | copy-start | bytes 196
where the time goes:
time: 46.8 us; the launch traced here: 46.7 us
  Pallas kernels  43.7 us (93%)
  local copies, waits for them, and re-layouts  2.94 us (6%)
    pallas_call x1, Pallas kernels, local(): pl.pallas_call(kernel, out_shape=jax.ShapeDtypeStruct(flow_state.shape, f...  43.7 us
    unnamed x7, local copies, waits for them, and re-layouts  2.94 us

commit v1 on v0

--- a/solution.py
+++ b/solution.py
@@ -10,10 +10,24 @@
 NZ = 32
 SX = 32
 SY = 16
-TY = 8
+VMEM_LIMIT = 56 * 1024 * 1024
 MAIN = 801.0
 GROUPS = ((0, (0,)), (2, (4,)), (1, (1, 2)), (1, (3,)))
 MESH = pl.DeviceIdType.MESH
+
+
+def far_first(*lengths):
+    offsets = [()]
+    for length in lengths:
+        offsets = [(*offset, k) for offset in offsets for k in range(length)]
+    hops = {
+        offset: sum(min(k, length - k) for k, length in zip(offset, lengths)) for offset in offsets
+    }
+    return sorted((offset for offset in offsets if any(offset)), key=lambda o: (-hops[o], o))
+
+
+X_ORDER = far_first(8, 4)
+Y_ORDER = far_first(8, 2)
 
 
 def roll(value, shift, axis):
@@ -222,6 +236,69 @@
     return d, joined_last, joined_first
 
 
+def y_weights(segments):
+    n = len(segments)
+    ones = jnp.ones_like(segments[0][0])
+    zero = jnp.zeros_like(ones)
+    den, high, a, c = [], [], [], []
+    for j, (to_before, to_after, _, _) in enumerate(segments):
+        after = segments[j + 1] if j < n - 1 else (zero,) * 4
+        den.append(1.0 / (1.0 - to_after * after[2]))
+        high.append(to_after * den[j])
+        a.append(to_before * den[j])
+        c.append(high[j] * after[3])
+    left, right = [None] * n, [None] * n
+    for j in range(n):
+        left[j] = c[j] / (1.0 - a[j] * left[j - 1]) if j else c[j]
+    for j in range(n - 1, -1, -1):
+        right[j] = a[j] / (1.0 - c[j] * right[j + 1]) if j < n - 1 else a[j]
+    gain = []
+    for j in range(n):
+        rest = ones
+        rest = rest - a[j] * left[j - 1] if j else rest
+        rest = rest - c[j] * right[j + 1] if j < n - 1 else rest
+        gain.append(1.0 / rest)
+    down, up = [ones] * n, [ones] * n
+    for j in range(1, n):
+        down[j] = down[j - 1] * right[j]
+    for j in range(n - 2, -1, -1):
+        up[j] = up[j + 1] * left[j]
+    weights = []
+    for j in range(n):
+        own_last = gain[j] * den[j]
+        own_first = right[j] * gain[j - 1] * high[j - 1] if j else zero
+        before_last = left[j - 1] * own_last if j else zero
+        before_first = gain[j - 1] * high[j - 1] if j else zero
+        down_inv = 1.0 / down[j]
+        up_inv = 1.0 / up[j - 1] if j else ones
+        weights.append(
+            (
+                own_last,
+                own_first,
+                before_last,
+                before_first,
+                down_inv,
+                up_inv,
+                down[j - 1] if j else zero,
+                up[j],
+                right[j],
+                left[j - 1] if j else zero,
+            )
+        )
+    return weights
+
+
+def y_emit(last, first, w):
+    own = w[0] * last + w[1] * first
+    before = w[2] * last + w[3] * first
+    return own, before, own * w[4], before * w[5]
+
+
+def y_meet(below, above, own, before, w):
+    low, high = w[6] * below, w[7] * above
+    return low + w[9] * high + before, w[8] * low + own + high
+
+
 def increments(s, prim, r, half_rc_inv, c2_inv):
     inv, u, v, w, p, c2, c = prim
     dp = 0.5 * (s[0] + s[4])
@@ -288,7 +365,6 @@
     out,
     q_sc,
     part_sc,
-    out_sc,
     speed_sc,
     x_send,
     x_low,
@@ -302,14 +378,17 @@
     xs_out,
     xs_in,
     ym_out,
-    yr_out,
     ym_in,
-    yr_in,
-    ys_out,
-    ys_in,
-    y_levels,
+    y_weight_sc,
+    y_weight,
+    yr_sc,
+    yf_out,
+    yf_in,
+    ys_sc,
+    x_code_sc,
+    y_code_sc,
     in_sem,
-    out_sem,
+    code_sem,
     halo_send,
     halo_recv,
     send_sem,
@@ -323,6 +402,12 @@
         pltpu.make_async_copy(
             flow.at[:, :, pl.ds(128 * b, 128)], q_sc.at[:, pl.ds(8 * b, 8), :], in_sem
         ).start()
+    code_copies = [
+        pltpu.make_async_copy(x_codes, x_code_sc, code_sem.at[0]),
+        pltpu.make_async_copy(y_codes, y_code_sc, code_sem.at[1]),
+    ]
+    for copy in code_copies:
+        copy.start()
 
     barrier = pltpu.get_barrier_semaphore()
 
@@ -341,6 +426,8 @@
     lax.fori_loop(1, SX, greet_x, 0)
     lax.fori_loop(1, SY, greet_y, 0)
     wait_all(q_sc, in_sem)
+    for copy in code_copies:
+        copy.wait()
 
     x_send[0] = q_sc[:, pl.ds(7, 8, stride=8), :]
     x_send[1] = q_sc[:, pl.ds(0, 8, stride=8), :]
@@ -371,8 +458,8 @@
         mine = pl.ds(gx * 4, 4)
         pltpu.make_async_copy(source.at[mine], target.at[mine], recv_sem.at[slot]).start()
 
-        def one(k, carry):
-            other = lax.rem(gx + k, SX)
+        for dy, dx in X_ORDER:
+            other = 4 * lax.rem(lax.div(gx, 4) + dy, 8) + lax.rem(lax.rem(gx, 4) + dx, 4)
             pltpu.make_async_remote_copy(
                 src_ref=source.at[pl.ds(other * 4, 4)],
                 dst_ref=target.at[mine],
@@ -381,35 +468,10 @@
                 device_id=(other, gy),
                 device_id_type=MESH,
             ).start()
-            return carry
-
-        lax.fori_loop(1, SX, one, 0)
-
-    solver_y = lax.rem(gy, 2) == 0
-    tile_y = lax.div(gy, 2)
-
-    def send_y(source, target, slot):
-        @pl.when(solver_y)
-        def _():
-            pltpu.make_async_copy(
-                source.at[pl.ds(tile_y * 4, 4)], target.at[pl.ds(gy * 4, 4)], recv_sem.at[slot]
-            ).start()
-
-        def one(t, carry):
-            @pl.when(gy != 2 * t)
-            def _():
-                pltpu.make_async_remote_copy(
-                    src_ref=source.at[pl.ds(t * 4, 4)],
-                    dst_ref=target.at[pl.ds(gy * 4, 4)],
-                    send_sem=send_sem.at[slot],
-                    recv_sem=recv_sem.at[slot],
-                    device_id=(gx, 2 * t),
-                    device_id_type=MESH,
-                ).start()
-
-            return carry
-
-        lax.fori_loop(0, TY, one, 0)
+
+    def others_y():
+        for dz, dc in Y_ORDER:
+            yield 2 * lax.rem(lax.div(gy, 2) + dz, 8) + lax.rem(lax.rem(gy, 2) + dc, 2)
 
     for copy in copies:
         copy.wait_recv()
@@ -419,7 +481,7 @@
     q = jnp.stack([low] + inner + [high], axis=1)
     prim_all = primitives(q)
 
-    lower, upper, first, last = x_bands(prim_all[1], prim_all[6], x_codes[...], start_x, end_x)
+    lower, upper, first, last = x_bands(prim_all[1], prim_all[6], x_code_sc[...], start_x, end_x)
     xm, xg, xp, xq, x_own = eliminate(lower, upper, first, last)
     for group, (matrix, families) in enumerate(GROUPS):
         for row in range(4):
@@ -451,16 +513,26 @@
 
     speeds = jnp.stack([speed_sc[:, pl.ds(k, 8, stride=8), :] for k in range(8)], axis=1)
     y_lower, y_upper = y_bands(swap_groups(speeds))
-    y_lower, y_upper, first, last = y_ends(y_lower, y_upper, y_codes[...], start_y, end_y)
+    y_lower, y_upper, first, last = y_ends(y_lower, y_upper, y_code_sc[...], start_y, end_y)
     ym, yg, yp, yq, y_own = eliminate(y_lower, y_upper, first, last)
     y_den, y_high_part, y_lev, y_p, y_q, y_joint, joined = y_join(y_own)
-    for group, (matrix, families) in enumerate(GROUPS):
-        for h in range(2):
-            at = (group * 2 + h) * 4
-            for row in range(4):
-                line = 7 if row < 2 else 0
-                ym_out[pl.ds(at + row, 1), :] = joined[row][matrix, h, line : line + 1]
-    send_y(ym_out, ym_in, 3)
+    ym_out[...] = jnp.zeros((32, 128), jnp.float32)
+    for kind in range(4):
+        line = 7 if kind < 2 else 0
+        for matrix in range(3):
+            for h in range(2):
+                at = kind * 8 + matrix * 2 + h
+                ym_out[pl.ds(at, 1), :] = joined[kind][matrix, h, line : line + 1]
+    pltpu.make_async_copy(ym_out, ym_in.at[gy], recv_sem.at[3]).start()
+    for other in others_y():
+        pltpu.make_async_remote_copy(
+            src_ref=ym_out,
+            dst_ref=ym_in.at[gy],
+            send_sem=send_sem.at[3],
+            recv_sem=recv_sem.at[3],
+            device_id=(gx, other),
+            device_id_type=MESH,
+        ).start()
 
     wait_all(xm_in, recv_sem.at[0])
     den, high_part, a, c = factor([xm_in[pl.ds(row, SX, stride=4), :] for row in range(4)])
@@ -475,14 +547,16 @@
         xs_out[pl.ds(2 * i + 1, SX, stride=4), :] = d
     send_x(xs_out, xs_in, 2)
 
-    @pl.when(solver_y)
-    def _():
-        wait_all(ym_in, recv_sem.at[3])
-        den, high_part, a, c = factor([ym_in[pl.ds(row, SY, stride=4), :] for row in range(4)])
-        y_levels[0], y_levels[1] = den, high_part
-        for i, level in enumerate(factor_levels(a, c)):
-            for j in range(3):
-                y_levels[2 + 3 * i + j] = level[j]
+    wait_all(ym_in, recv_sem.at[3])
+    segments = [
+        tuple(ym_in[j, pl.ds(8 * kind, 8), :] for kind in range(4)) for j in range(SY)
+    ]
+    for j, weights in enumerate(y_weights(segments)):
+        for i, weight in enumerate(weights):
+            y_weight_sc[j, i] = weight
+    for i in range(10):
+        for family, matrix in enumerate((0, 1, 1, 1, 2)):
+            y_weight[i, pl.ds(2 * family, 2), :] = y_weight_sc[gy, i, pl.ds(2 * matrix, 2), :]
 
     r = q[0, 1:9]
     rc = r * prim[6]
@@ -503,56 +577,35 @@
     y_d, joined_last, joined_first = y_join_right(
         yd[0], y_last, y_own, y_den, y_high_part, y_lev, y_joint
     )
-    line_zero = jnp.zeros((1, 128), jnp.float32)
-    for group, (matrix, families) in enumerate(GROUPS):
+    for family in range(5):
         for h in range(2):
-            for i in range(2):
-                at = (group * 2 + h) * 4 + 2 * i
-                some = i < len(families)
-                yr_out[pl.ds(at, 1), :] = joined_last[families[i], h, 7:8] if some else line_zero
-                yr_out[pl.ds(at + 1, 1), :] = (
-                    joined_first[families[i], h, 0:1] if some else line_zero
-                )
-    send_y(yr_out, yr_in, 4)
-
-    @pl.when(solver_y)
-    def _():
-        wait_all(yr_in, recv_sem.at[4])
-        levels = [tuple(y_levels[2 + 3 * i + j] for j in range(3)) for i in range(4)]
-        for i in range(2):
-            own_last = yr_in[pl.ds(2 * i, SY, stride=4), :]
-            own_first = yr_in[pl.ds(2 * i + 1, SY, stride=4), :]
-            d = y_levels[0] * own_last + y_levels[1] * roll(own_first, -1, 0)
-            d = reduce_levels(d, levels)
-            ys_out[pl.ds(2 * i, SY, stride=4), :] = roll(d, 1, 0)
-            ys_out[pl.ds(2 * i + 1, SY, stride=4), :] = d
-        pltpu.make_async_copy(
-            ys_out.at[pl.ds(gy * 4, 4)], ys_in.at[pl.ds(tile_y * 4, 4)], recv_sem.at[5]
+            yr_sc[0, pl.ds(2 * family + h, 1), :] = joined_last[family, h, 7:8]
+            yr_sc[1, pl.ds(2 * family + h, 1), :] = joined_first[family, h, 0:1]
+    weights = [y_weight[i] for i in range(10)]
+    own_add, before_add, own_out, before_out = y_emit(yr_sc[0], yr_sc[1], weights)
+    yf_out[0], yf_out[1] = own_out, before_out
+    for other in others_y():
+        pltpu.make_async_remote_copy(
+            src_ref=yf_out.at[jnp.where(other < gy, 1, 0), pl.ds(0, 10)],
+            dst_ref=yf_in.at[gy, pl.ds(0, 10)],
+            send_sem=send_sem.at[4],
+            recv_sem=recv_sem.at[4],
+            device_id=(gx, other),
+            device_id_type=MESH,
         ).start()
-
-        def one(k, carry):
-            other = lax.rem(gy + k, SY)
-            pltpu.make_async_remote_copy(
-                src_ref=ys_out.at[pl.ds(other * 4, 4)],
-                dst_ref=ys_in.at[pl.ds(tile_y * 4, 4)],
-                send_sem=send_sem.at[5],
-                recv_sem=recv_sem.at[5],
-                device_id=(gx, other),
-                device_id_type=MESH,
-            ).start()
-            return carry
-
-        lax.fori_loop(1, SY, one, 0)
-
-    wait_all(ys_in, recv_sem.at[5])
+    wait_all(yf_in.at[pl.ds(0, SY - 1), pl.ds(0, 10)], recv_sem.at[4])
+    zero = jnp.zeros((16, 128), jnp.float32)
+    below = sum((jnp.where(j < gy, yf_in[j], 0.0) for j in range(SY - 1)), zero)
+    above = sum((jnp.where(j > gy, yf_in[j], 0.0) for j in range(1, SY)), zero)
+    ys_sc[0], ys_sc[1] = y_meet(below, above, own_add, before_add, weights)
 
     def y_value(kind):
-        rows = []
-        for group, i in ((0, 0), (2, 0), (2, 1), (3, 0), (1, 0)):
-            rows.append(
-                jnp.stack([ys_in[pl.ds((group * 2 + h) * 4 + 2 * i + kind, 1), :] for h in range(2)])
-            )
-        return jnp.stack(rows)
+        return jnp.stack(
+            [
+                jnp.stack([ys_sc[kind, pl.ds(2 * family + h, 1), :] for h in range(2)])
+                for family in range(5)
+            ]
+        )
 
     before, own = y_value(0), y_value(1)
     groups = y_d + five(y_p) * before + five(y_q) * own
@@ -561,29 +614,14 @@
     solved = swap_groups(solved.reshape(5, 8, 8, 128))
     for field, value in enumerate(increments(solved, prim, r, half_rc_inv, c2_inv)):
         for k in range(8):
-            out_sc[field, pl.ds(k, 8, stride=8), :] = value[k]
-    for b in range(8):
-        pltpu.make_async_copy(
-            out_sc.at[:, pl.ds(8 * b, 8), :], out.at[:, :, pl.ds(128 * b, 128)], out_sem
-        ).start()
+            out[field, pl.ds(k, 8, stride=8), :] = value[k]
 
     for copy in copies:
         copy.wait_send()
     for slot in range(3):
         wait_all(xm_out.at[pl.ds(0, 4 * (SX - 1))], send_sem.at[slot])
-
-    @pl.when(solver_y)
-    def _():
-        for slot in (3, 4):
-            wait_all(ym_out.at[pl.ds(0, 4 * (TY - 1))], send_sem.at[slot])
-        wait_all(ys_out.at[pl.ds(0, 4 * (SY - 1))], send_sem.at[5])
-
-    @pl.when(jnp.logical_not(solver_y))
-    def _():
-        for slot in (3, 4):
-            wait_all(ym_out, send_sem.at[slot])
-
-    wait_all(out_sc, out_sem)
+    wait_all(ym_in.at[pl.ds(0, SY - 1)], send_sem.at[3])
+    wait_all(yf_in.at[pl.ds(0, SY - 1), pl.ds(0, 10)], send_sem.at[4])
 
 
 def local(flow_state, x_codes, y_codes):
@@ -592,17 +630,12 @@
     def vmem(*shape):
         return pltpu.VMEM(shape, f32)
 
-    return pl.pallas_call(
+    result = pl.pallas_call(
         kernel,
-        out_shape=jax.ShapeDtypeStruct(flow_state.shape, f32),
-        in_specs=[
-            pl.BlockSpec(memory_space=pl.ANY),
-            pl.BlockSpec(memory_space=pltpu.VMEM),
-            pl.BlockSpec(memory_space=pltpu.VMEM),
-        ],
-        out_specs=pl.BlockSpec(memory_space=pl.ANY),
+        out_shape=jax.ShapeDtypeStruct((5, 64, 128), f32),
+        in_specs=[pl.BlockSpec(memory_space=pltpu.HBM)] * 3,
+        out_specs=pl.BlockSpec(memory_space=pltpu.VMEM),
         scratch_shapes=[
-            vmem(5, 64, 128),
             vmem(5, 64, 128),
             vmem(5, 64, 128),
             vmem(4, 64, 128),
@@ -617,25 +650,30 @@
             vmem(4 * SX, 128),
             vmem(4 * SX, 128),
             vmem(4 * SX, 128),
-            vmem(4 * TY, 128),
-            vmem(4 * TY, 128),
-            vmem(4 * SY, 128),
-            vmem(4 * SY, 128),
-            vmem(4 * SY, 128),
-            vmem(4 * TY, 128),
-            vmem(14, SY, 128),
+            vmem(32, 128),
+            vmem(SY, 32, 128),
+            vmem(SY, 10, 8, 128),
+            vmem(10, 16, 128),
+            vmem(2, 16, 128),
+            vmem(2, 16, 128),
+            vmem(SY, 16, 128),
+            vmem(2, 16, 128),
+            pltpu.VMEM((2, 32), jnp.int32),
+            pltpu.VMEM((2, 8), jnp.int32),
             pltpu.SemaphoreType.DMA,
-            pltpu.SemaphoreType.DMA,
+            pltpu.SemaphoreType.DMA((2,)),
             pltpu.SemaphoreType.DMA((4,)),
             pltpu.SemaphoreType.DMA((4,)),
-            pltpu.SemaphoreType.DMA((6,)),
-            pltpu.SemaphoreType.DMA((6,)),
+            pltpu.SemaphoreType.DMA((5,)),
+            pltpu.SemaphoreType.DMA((5,)),
         ],
         compiler_params=pltpu.CompilerParams(
-            collective_id=0, has_side_effects=True, vmem_limit_bytes=32 * 1024 * 1024
+            collective_id=0, has_side_effects=True, vmem_limit_bytes=VMEM_LIMIT
         ),
         name="step",
     )(flow_state, x_codes, y_codes)
+    result = jnp.transpose(result.reshape(5, 8, 8, 128), (0, 2, 1, 3))
+    return result.reshape(flow_state.shape)
 
 
 def solution(mesh):

time: 46.8 us -> 40.6 us (0.87)
  Pallas kernels: 43.7 us -> 38.8 us
  local copies, waits for them, and re-layouts: 2.94 us -> 1.59 us
    pallas_call x1, Pallas kernels: 43.7 us -> 38.8 us  [local(): pl.pallas_call(kernel, out_shape=jax.ShapeDtypeStruct((5, 64, 128), f32),...]
    unnamed x7 -> x1, local copies, waits for them, and re-layouts: 2.94 us -> 1.59 us
where the time goes in v1:
time: 40.6 us; the launch traced here: 40.4 us
  Pallas kernels  38.8 us (96%)
  local copies, waits for them, and re-layouts  1.59 us (4%)
    pallas_call x1, Pallas kernels, local(): pl.pallas_call(kernel, out_shape=jax.ShapeDtypeStruct((5, 64, 128), f32),...  38.8 us
    unnamed x1, local copies, waits for them, and re-layouts  1.59 us

profile of v1, /device:TPU:1, one launch (start us, length us, event | category | flops | bytes accessed | tf_op | source)
XLA Modules:
  0.0 40.4 jit_solution(7716652542368270169)
XLA Ops:
  0.0 38.8 %step.1 = f32[5,64,128]{2,1,0:T(8,128)} custom-call(f32[5,8,1024]{2,1,0:T(8,128)} %flow.1, s32[2,32]{1,0:T(2,128)} %x_codes.1, s32[2,8]{1,0:T(2,128)} %y_codes.1), custom_call_target="tpu_custom_call" | custom-call | tf_op jit(solution)/shard_map/step/pallas_call | solution.py:633
  38.8 1.6 %copy.5 = f32[5,8,1024]{2,1,0:T(8,128)} copy(f32[5,8,1024]{2,1,0:T(8,128)} %bitcast.5) | data formatting | bytes 327680

commit v2 on v1

--- a/solution.py
+++ b/solution.py
@@ -387,6 +387,7 @@
     ys_sc,
     x_code_sc,
     y_code_sc,
+    word,
     in_sem,
     code_sem,
     halo_send,
@@ -409,32 +410,37 @@
     for copy in code_copies:
         copy.start()
 
+    chip_y, chip_x = lax.div(gx, 4), lax.rem(gx, 4)
+    chip_z, core = lax.div(gy, 2), lax.rem(gy, 2)
+    x_after, x_before = lax.rem(gx + 1, SX), lax.rem(gx + SX - 1, SX)
+    y_after, y_before = lax.rem(gy + 1, SY), lax.rem(gy + SY - 1, SY)
+    ring = [
+        (4 * lax.rem(chip_y + 1, 8) + chip_x, gy),
+        (4 * lax.rem(chip_y + 7, 8) + chip_x, gy),
+        (gx, 2 * lax.rem(chip_z + 1, 8) + core),
+        (gx, 2 * lax.rem(chip_z + 7, 8) + core),
+    ]
+    near = [(4 * chip_y + lax.rem(chip_x + k, 4), gy) for k in range(1, 4)]
+    near += [(gx, 2 * chip_z + 1 - core), (gx, y_after), (gx, y_before)]
+    near += [(x_after, gy), (x_before, gy)] + ring
     barrier = pltpu.get_barrier_semaphore()
-
-    def greet_x(k, carry):
-        pl.semaphore_signal(
-            barrier, inc=1, device_id=(lax.rem(gx + k, SX), gy), device_id_type=MESH
-        )
-        return carry
-
-    def greet_y(k, carry):
-        pl.semaphore_signal(
-            barrier, inc=1, device_id=(gx, lax.rem(gy + k, SY)), device_id_type=MESH
-        )
-        return carry
-
-    lax.fori_loop(1, SX, greet_x, 0)
-    lax.fori_loop(1, SY, greet_y, 0)
+    for device in near:
+        pl.semaphore_signal(barrier, inc=1, device_id=device, device_id_type=MESH)
+
+    def tell(step):
+        for device in ring:
+            pl.semaphore_signal(word.at[step], inc=1, device_id=device, device_id_type=MESH)
+
+    def heard(step):
+        pl.semaphore_wait(word.at[step], len(ring))
+
     wait_all(q_sc, in_sem)
     for copy in code_copies:
         copy.wait()
 
     x_send[0] = q_sc[:, pl.ds(7, 8, stride=8), :]
     x_send[1] = q_sc[:, pl.ds(0, 8, stride=8), :]
-    pl.semaphore_wait(barrier, SX + SY - 2)
-
-    x_after, x_before = lax.rem(gx + 1, SX), lax.rem(gx + SX - 1, SX)
-    y_after, y_before = lax.rem(gy + 1, SY), lax.rem(gy + SY - 1, SY)
+    pl.semaphore_wait(barrier, len(near))
     halos = [
         (x_send.at[0], x_low, (x_after, gy)),
         (x_send.at[1], x_high, (x_before, gy)),
@@ -453,6 +459,10 @@
         )
         copy.start()
         copies.append(copy)
+    for step in range(3):
+        tell(step)
+        heard(step)
+    tell(3)
 
     def send_x(source, target, slot):
         mine = pl.ds(gx * 4, 4)
@@ -486,6 +496,7 @@
     for group, (matrix, families) in enumerate(GROUPS):
         for row in range(4):
             xm_out[pl.ds(group * 32 + row, 8, stride=4), :] = x_own[row][matrix]
+    heard(3)
     send_x(xm_out, xm_in, 0)
 
     blocks = q_sc[...].reshape(5, 8, 8, 128)
@@ -660,6 +671,7 @@
             vmem(2, 16, 128),
             pltpu.VMEM((2, 32), jnp.int32),
             pltpu.VMEM((2, 8), jnp.int32),
+            pltpu.SemaphoreType.REGULAR((4,)),
             pltpu.SemaphoreType.DMA,
             pltpu.SemaphoreType.DMA((2,)),
             pltpu.SemaphoreType.DMA((4,)),

time: 40.6 us -> 40.4 us (level)
  no operation moved by 1% of the time
where the time goes in v2:
time: 40.4 us; the launch traced here: 40.2 us
  Pallas kernels  38.6 us (96%)
  local copies, waits for them, and re-layouts  1.59 us (4%)
    pallas_call x1, Pallas kernels, local(): pl.pallas_call(kernel, out_shape=jax.ShapeDtypeStruct((5, 64, 128), f32),...  38.6 us
    unnamed x1, local copies, waits for them, and re-layouts  1.59 us

profile of v2, /device:TPU:1, one launch (start us, length us, event | category | flops | bytes accessed | tf_op | source)
XLA Modules:
  0.0 40.2 jit_solution(1642295165715625045)
XLA Ops:
  0.0 38.6 %step.1 = f32[5,64,128]{2,1,0:T(8,128)} custom-call(f32[5,8,1024]{2,1,0:T(8,128)} %flow.1, s32[2,32]{1,0:T(2,128)} %x_codes.1, s32[2,8]{1,0:T(2,128)} %y_codes.1), custom_call_target="tpu_custom_call" | custom-call | tf_op jit(solution)/shard_map/step/pallas_call | solution.py:644
  38.6 1.6 %copy.5 = f32[5,8,1024]{2,1,0:T(8,128)} copy(f32[5,8,1024]{2,1,0:T(8,128)} %bitcast.5) | data formatting | bytes 327680

commit v3 on v2

--- a/solution.py
+++ b/solution.py
@@ -26,6 +26,7 @@
     return sorted((offset for offset in offsets if any(offset)), key=lambda o: (-hops[o], o))
 
 
+NEAR = (0, 1, 7)
 X_ORDER = far_first(8, 4)
 Y_ORDER = far_first(8, 2)
 
@@ -414,25 +415,26 @@
     chip_z, core = lax.div(gy, 2), lax.rem(gy, 2)
     x_after, x_before = lax.rem(gx + 1, SX), lax.rem(gx + SX - 1, SX)
     y_after, y_before = lax.rem(gy + 1, SY), lax.rem(gy + SY - 1, SY)
-    ring = [
-        (4 * lax.rem(chip_y + 1, 8) + chip_x, gy),
-        (4 * lax.rem(chip_y + 7, 8) + chip_x, gy),
-        (gx, 2 * lax.rem(chip_z + 1, 8) + core),
-        (gx, 2 * lax.rem(chip_z + 7, 8) + core),
-    ]
-    near = [(4 * chip_y + lax.rem(chip_x + k, 4), gy) for k in range(1, 4)]
-    near += [(gx, 2 * chip_z + 1 - core), (gx, y_after), (gx, y_before)]
-    near += [(x_after, gy), (x_before, gy)] + ring
+
+    def x_at(dy, dx):
+        return 4 * lax.rem(chip_y + dy, 8) + lax.rem(chip_x + dx, 4), gy
+
+    def y_at(dz, dc):
+        return gx, 2 * lax.rem(chip_z + dz, 8) + lax.rem(core + dc, 2)
+
+    near = [x_at(dy, dx) for dy, dx in X_ORDER if dy in NEAR]
+    near += [y_at(dz, dc) for dz, dc in Y_ORDER if dz in NEAR]
     barrier = pltpu.get_barrier_semaphore()
     for device in near:
         pl.semaphore_signal(barrier, inc=1, device_id=device, device_id_type=MESH)
 
     def tell(step):
-        for device in ring:
-            pl.semaphore_signal(word.at[step], inc=1, device_id=device, device_id_type=MESH)
+        for k in (step + 1, 7 - step):
+            for device in (x_at(k, 0), y_at(k, 0)):
+                pl.semaphore_signal(word.at[step], inc=1, device_id=device, device_id_type=MESH)
 
     def heard(step):
-        pl.semaphore_wait(word.at[step], len(ring))
+        pl.semaphore_wait(word.at[step], 4)
 
     wait_all(q_sc, in_sem)
     for copy in code_copies:
@@ -459,10 +461,9 @@
         )
         copy.start()
         copies.append(copy)
-    for step in range(3):
-        tell(step)
-        heard(step)
-    tell(3)
+    tell(0)
+    heard(0)
+    tell(1)
 
     def send_x(source, target, slot):
         mine = pl.ds(gx * 4, 4)
@@ -496,7 +497,7 @@
     for group, (matrix, families) in enumerate(GROUPS):
         for row in range(4):
             xm_out[pl.ds(group * 32 + row, 8, stride=4), :] = x_own[row][matrix]
-    heard(3)
+    heard(1)
     send_x(xm_out, xm_in, 0)
 
     blocks = q_sc[...].reshape(5, 8, 8, 128)
@@ -671,7 +672,7 @@
             vmem(2, 16, 128),
             pltpu.VMEM((2, 32), jnp.int32),
             pltpu.VMEM((2, 8), jnp.int32),
-            pltpu.SemaphoreType.REGULAR((4,)),
+            pltpu.SemaphoreType.REGULAR((2,)),
             pltpu.SemaphoreType.DMA,
             pltpu.SemaphoreType.DMA((2,)),
             pltpu.SemaphoreType.DMA((4,)),

time: 40.4 us -> 38.6 us (0.955)
  Pallas kernels: 38.6 us -> 36.8 us
    pallas_call x1, Pallas kernels: 38.6 us -> 36.8 us  [local(): pl.pallas_call(kernel, out_shape=jax.ShapeDtypeStruct((5, 64, 128), f32),...]
where the time goes in v3:
time: 38.6 us; the launch traced here: 38.4 us
  Pallas kernels  36.8 us (95%)
  local copies, waits for them, and re-layouts  1.59 us (4%)
    pallas_call x1, Pallas kernels, local(): pl.pallas_call(kernel, out_shape=jax.ShapeDtypeStruct((5, 64, 128), f32),...  36.8 us
    unnamed x1, local copies, waits for them, and re-layouts  1.59 us

profile of v3, /device:TPU:1, one launch (start us, length us, event | category | flops | bytes accessed | tf_op | source)
XLA Modules:
  0.0 38.4 jit_solution(14435726914537411340)
XLA Ops:
  0.0 36.8 %step.1 = f32[5,64,128]{2,1,0:T(8,128)} custom-call(f32[5,8,1024]{2,1,0:T(8,128)} %flow.1, s32[2,32]{1,0:T(2,128)} %x_codes.1, s32[2,8]{1,0:T(2,128)} %y_codes.1), custom_call_target="tpu_custom_call" | custom-call | tf_op jit(solution)/shard_map/step/pallas_call | solution.py:645
  36.8 1.6 %copy.5 = f32[5,8,1024]{2,1,0:T(8,128)} copy(f32[5,8,1024]{2,1,0:T(8,128)} %bitcast.5) | data formatting | bytes 327680

commit v4 on v3

--- a/solution.py
+++ b/solution.py
@@ -10,7 +10,7 @@
 NZ = 32
 SX = 32
 SY = 16
-VMEM_LIMIT = 56 * 1024 * 1024
+VMEM_LIMIT = 54950 * 1024
 MAIN = 801.0
 GROUPS = ((0, (0,)), (2, (4,)), (1, (1, 2)), (1, (3,)))
 MESH = pl.DeviceIdType.MESH
@@ -73,27 +73,28 @@
     return after - before
 
 
-def yz_part(q):
-    inv, u, v, w, p, c2, c = primitives(q)
-    flux = jnp.stack([q[2], q[1] * v, q[2] * v + p, q[3] * v, v * (q[4] + p)])
+def y_terms(q, prim):
+    inv, u, v, w, p, c2, c = prim
+    flux = 0.25 * jnp.stack([q[2], q[1] * v, q[2] * v + p, q[3] * v, v * (q[4] + p)])
     smooth = 400.0 * q
-    flux = 0.25 * flux
-    inner, wi, pi = q[:, 1:9], w[1:9], p[1:9]
-    flux_z = jnp.stack(
-        [inner[3], inner[1] * wi, inner[2] * wi, inner[3] * wi + pi, wi * (inner[4] + pi)]
-    )
-    part = up_y(smooth - flux) + down_y(smooth + flux) - 1600.0 * inner
-    part = part - 0.25 * z_difference(flux_z)
-    speeds = jnp.stack([v, c])
-    return part, jnp.concatenate([down_y(speeds), up_y(speeds)])
-
-
-def x_part(q, prim):
+    return smooth - flux, smooth + flux, jnp.stack([v, c])
+
+
+def z_terms(q, prim):
     inv, u, v, w, p, c2, c = prim
-    flux = jnp.stack([q[1], q[1] * u + p, q[2] * u, q[3] * u, u * (q[4] + p)])
+    flux = jnp.stack([q[3], q[1] * w, q[2] * w, q[3] * w + p, w * (q[4] + p)])
+    return -1600.0 * q - 0.25 * z_difference(flux)
+
+
+def x_terms(q, prim):
+    inv, u, v, w, p, c2, c = prim
+    flux = 0.25 * jnp.stack([q[1], q[1] * u + p, q[2] * u, q[3] * u, u * (q[4] + p)])
     smooth = 400.0 * q
-    flux = 0.25 * flux
-    return (smooth - flux)[:, 2:10] + (smooth + flux)[:, 0:8]
+    return smooth - flux, smooth + flux
+
+
+def join(low, inner, high):
+    return jnp.concatenate([low[:, None], inner, high[:, None]], axis=1)
 
 
 def x_right(res, prim):
@@ -361,8 +362,7 @@
 
 def kernel(
     flow,
-    x_codes,
-    y_codes,
+    codes,
     out,
     q_sc,
     part_sc,
@@ -384,10 +384,11 @@
     y_weight,
     yr_sc,
     yf_out,
+    yc_in,
+    yb_out,
     yf_in,
     ys_sc,
-    x_code_sc,
-    y_code_sc,
+    code_sc,
     word,
     in_sem,
     code_sem,
@@ -400,17 +401,6 @@
     start_x, end_x = gx == 0, gx == SX - 1
     start_y, end_y = gy == 0, gy == SY - 1
 
-    for b in range(8):
-        pltpu.make_async_copy(
-            flow.at[:, :, pl.ds(128 * b, 128)], q_sc.at[:, pl.ds(8 * b, 8), :], in_sem
-        ).start()
-    code_copies = [
-        pltpu.make_async_copy(x_codes, x_code_sc, code_sem.at[0]),
-        pltpu.make_async_copy(y_codes, y_code_sc, code_sem.at[1]),
-    ]
-    for copy in code_copies:
-        copy.start()
-
     chip_y, chip_x = lax.div(gx, 4), lax.rem(gx, 4)
     chip_z, core = lax.div(gy, 2), lax.rem(gy, 2)
     x_after, x_before = lax.rem(gx + 1, SX), lax.rem(gx + SX - 1, SX)
@@ -428,6 +418,13 @@
     for device in near:
         pl.semaphore_signal(barrier, inc=1, device_id=device, device_id_type=MESH)
 
+    for b in range(8):
+        pltpu.make_async_copy(
+            flow.at[:, :, pl.ds(128 * b, 128)], q_sc.at[:, pl.ds(8 * b, 8), :], in_sem
+        ).start()
+    code_copy = pltpu.make_async_copy(codes, code_sc, code_sem)
+    code_copy.start()
+
     def tell(step):
         for k in (step + 1, 7 - step):
             for device in (x_at(k, 0), y_at(k, 0)):
@@ -436,13 +433,13 @@
     def heard(step):
         pl.semaphore_wait(word.at[step], 4)
 
+    pl.semaphore_wait(barrier, len(near))
+    tell(0)
     wait_all(q_sc, in_sem)
-    for copy in code_copies:
-        copy.wait()
+    code_copy.wait()
 
     x_send[0] = q_sc[:, pl.ds(7, 8, stride=8), :]
     x_send[1] = q_sc[:, pl.ds(0, 8, stride=8), :]
-    pl.semaphore_wait(barrier, len(near))
     halos = [
         (x_send.at[0], x_low, (x_after, gy)),
         (x_send.at[1], x_high, (x_before, gy)),
@@ -461,7 +458,6 @@
         )
         copy.start()
         copies.append(copy)
-    tell(0)
     heard(0)
     tell(1)
 
@@ -484,15 +480,24 @@
         for dz, dc in Y_ORDER:
             yield 2 * lax.rem(lax.div(gy, 2) + dz, 8) + lax.rem(lax.rem(gy, 2) + dc, 2)
 
+    blocks = q_sc[...].reshape(5, 8, 8, 128)
+    prim_o = primitives(blocks)
+    to_before_y, to_after_y, speeds_y = y_terms(blocks, prim_o)
+    part_z = z_terms(blocks, prim_o)
+    q = jnp.stack([q_sc[:, pl.ds(k, 8, stride=8), :] for k in range(8)], axis=1)
+    prim = primitives(q)
+    to_before_x, to_after_x = x_terms(q, prim)
+
     for copy in copies:
         copy.wait_recv()
-    inner = [q_sc[:, pl.ds(k, 8, stride=8), :] for k in range(8)]
-    low = jnp.where(start_x, inner[0], x_low[...])
-    high = jnp.where(end_x, inner[7], x_high[...])
-    q = jnp.stack([low] + inner + [high], axis=1)
-    prim_all = primitives(q)
-
-    lower, upper, first, last = x_bands(prim_all[1], prim_all[6], x_code_sc[...], start_x, end_x)
+    low = jnp.where(start_x, q[:, 0], x_low[...])
+    high = jnp.where(end_x, q[:, 7], x_high[...])
+    prim_low, prim_high = primitives(low), primitives(high)
+    u, c = (
+        jnp.concatenate([prim_low[i][None], prim[i], prim_high[i][None]]) for i in (1, 6)
+    )
+
+    lower, upper, first, last = x_bands(u, c, code_sc[:, 0:32], start_x, end_x)
     xm, xg, xp, xq, x_own = eliminate(lower, upper, first, last)
     for group, (matrix, families) in enumerate(GROUPS):
         for row in range(4):
@@ -500,17 +505,20 @@
     heard(1)
     send_x(xm_out, xm_in, 0)
 
-    blocks = q_sc[...].reshape(5, 8, 8, 128)
     y_edge_low = jnp.where(start_y, roll(blocks[:, 0], 96, -1), y_low[...])
     y_edge_high = jnp.where(end_y, roll(blocks[:, 7], 32, -1), y_high[...])
-    part, speeds = yz_part(
-        jnp.concatenate([y_edge_low[:, None], blocks, y_edge_high[:, None]], axis=1)
+    low_terms = y_terms(y_edge_low, primitives(y_edge_low))
+    high_terms = y_terms(y_edge_high, primitives(y_edge_high))
+    part = (
+        up_y(join(low_terms[0], to_before_y, high_terms[0]))
+        + down_y(join(low_terms[1], to_after_y, high_terms[1]))
+        + part_z
     )
     part_sc[...] = part.reshape(5, 64, 128)
-    speed_sc[...] = speeds.reshape(4, 64, 128)
-    prim = tuple(value[1:9] for value in prim_all)
-    residual = x_part(q, prim_all) + jnp.stack(
-        [part_sc[:, pl.ds(k, 8, stride=8), :] for k in range(8)], axis=1
+    residual = (
+        jnp.concatenate([to_before_x[:, 1:], x_terms(high, prim_high)[0][:, None]], axis=1)
+        + jnp.concatenate([x_terms(low, prim_low)[1][:, None], to_after_x[:, :7]], axis=1)
+        + jnp.stack([part_sc[:, pl.ds(k, 8, stride=8), :] for k in range(8)], axis=1)
     )
     right = x_right(residual, prim)
     xd, x_last = eliminate_right([right[:, k] for k in range(8)], lower, xm, xg)
@@ -523,9 +531,11 @@
             xr_out[pl.ds(at + 1, 8, stride=4), :] = xd[0][families[i]] if some else zero
     send_x(xr_out, xr_in, 1)
 
+    speeds_y = join(low_terms[2], speeds_y, high_terms[2])
+    speed_sc[...] = jnp.concatenate([down_y(speeds_y), up_y(speeds_y)]).reshape(4, 64, 128)
     speeds = jnp.stack([speed_sc[:, pl.ds(k, 8, stride=8), :] for k in range(8)], axis=1)
     y_lower, y_upper = y_bands(swap_groups(speeds))
-    y_lower, y_upper, first, last = y_ends(y_lower, y_upper, y_code_sc[...], start_y, end_y)
+    y_lower, y_upper, first, last = y_ends(y_lower, y_upper, code_sc[:, 32:40], start_y, end_y)
     ym, yg, yp, yq, y_own = eliminate(y_lower, y_upper, first, last)
     y_den, y_high_part, y_lev, y_p, y_q, y_joint, joined = y_join(y_own)
     ym_out[...] = jnp.zeros((32, 128), jnp.float32)
@@ -570,7 +580,7 @@
         for family, matrix in enumerate((0, 1, 1, 1, 2)):
             y_weight[i, pl.ds(2 * family, 2), :] = y_weight_sc[gy, i, pl.ds(2 * matrix, 2), :]
 
-    r = q[0, 1:9]
+    r = q[0]
     rc = r * prim[6]
     half_rc_inv = 0.5 / rc
     c2_inv = 1.0 / prim[5]
@@ -596,19 +606,34 @@
     weights = [y_weight[i] for i in range(10)]
     own_add, before_add, own_out, before_out = y_emit(yr_sc[0], yr_sc[1], weights)
     yf_out[0], yf_out[1] = own_out, before_out
-    for other in others_y():
-        pltpu.make_async_remote_copy(
-            src_ref=yf_out.at[jnp.where(other < gy, 1, 0), pl.ds(0, 10)],
-            dst_ref=yf_in.at[gy, pl.ds(0, 10)],
-            send_sem=send_sem.at[4],
-            recv_sem=recv_sem.at[4],
-            device_id=(gx, other),
-            device_id_type=MESH,
-        ).start()
-    wait_all(yf_in.at[pl.ds(0, SY - 1), pl.ds(0, 10)], recv_sem.at[4])
-    zero = jnp.zeros((16, 128), jnp.float32)
-    below = sum((jnp.where(j < gy, yf_in[j], 0.0) for j in range(SY - 1)), zero)
-    above = sum((jnp.where(j > gy, yf_in[j], 0.0) for j in range(1, SY)), zero)
+    core_copy = pltpu.make_async_remote_copy(
+        src_ref=yf_out.at[:, pl.ds(0, 10)],
+        dst_ref=yc_in.at[:, pl.ds(0, 10)],
+        send_sem=send_sem.at[5],
+        recv_sem=recv_sem.at[5],
+        device_id=(gx, 2 * chip_z + 1 - core),
+        device_id_type=MESH,
+    )
+    core_copy.start()
+    core_copy.wait_recv()
+    yb_out[0], yb_out[1] = own_out + yc_in[0], before_out + yc_in[1]
+    for dz, dc in Y_ORDER:
+        if dc == 0:
+            other = lax.rem(chip_z + dz, 8)
+            pltpu.make_async_remote_copy(
+                src_ref=yb_out.at[jnp.where(other < chip_z, 1, 0), pl.ds(0, 10)],
+                dst_ref=yf_in.at[chip_z, pl.ds(0, 10)],
+                send_sem=send_sem.at[4],
+                recv_sem=recv_sem.at[4],
+                device_id=(gx, 2 * other + core),
+                device_id_type=MESH,
+            ).start()
+    below = jnp.where(core == 1, yc_in[0], 0.0)
+    above = jnp.where(core == 0, yc_in[1], 0.0)
+    wait_all(yf_in.at[pl.ds(0, 7), pl.ds(0, 10)], recv_sem.at[4])
+    for j in range(8):
+        below = below + jnp.where(j < chip_z, yf_in[j], 0.0)
+        above = above + jnp.where(j > chip_z, yf_in[j], 0.0)
     ys_sc[0], ys_sc[1] = y_meet(below, above, own_add, before_add, weights)
 
     def y_value(kind):
@@ -633,7 +658,8 @@
     for slot in range(3):
         wait_all(xm_out.at[pl.ds(0, 4 * (SX - 1))], send_sem.at[slot])
     wait_all(ym_in.at[pl.ds(0, SY - 1)], send_sem.at[3])
-    wait_all(yf_in.at[pl.ds(0, SY - 1), pl.ds(0, 10)], send_sem.at[4])
+    wait_all(yf_in.at[pl.ds(0, 7), pl.ds(0, 10)], send_sem.at[4])
+    core_copy.wait_send()
 
 
 def local(flow_state, x_codes, y_codes):
@@ -645,7 +671,7 @@
     result = pl.pallas_call(
         kernel,
         out_shape=jax.ShapeDtypeStruct((5, 64, 128), f32),
-        in_specs=[pl.BlockSpec(memory_space=pltpu.HBM)] * 3,
+        in_specs=[pl.BlockSpec(memory_space=pl.ANY)] * 2,
         out_specs=pl.BlockSpec(memory_space=pltpu.VMEM),
         scratch_shapes=[
             vmem(5, 64, 128),
@@ -668,23 +694,24 @@
             vmem(10, 16, 128),
             vmem(2, 16, 128),
             vmem(2, 16, 128),
-            vmem(SY, 16, 128),
             vmem(2, 16, 128),
-            pltpu.VMEM((2, 32), jnp.int32),
-            pltpu.VMEM((2, 8), jnp.int32),
+            vmem(2, 16, 128),
+            vmem(8, 16, 128),
+            vmem(2, 16, 128),
+            pltpu.VMEM((2, 40), jnp.int32),
             pltpu.SemaphoreType.REGULAR((2,)),
             pltpu.SemaphoreType.DMA,
-            pltpu.SemaphoreType.DMA((2,)),
+            pltpu.SemaphoreType.DMA,
             pltpu.SemaphoreType.DMA((4,)),
             pltpu.SemaphoreType.DMA((4,)),
-            pltpu.SemaphoreType.DMA((5,)),
-            pltpu.SemaphoreType.DMA((5,)),
+            pltpu.SemaphoreType.DMA((6,)),
+            pltpu.SemaphoreType.DMA((6,)),
         ],
         compiler_params=pltpu.CompilerParams(
             collective_id=0, has_side_effects=True, vmem_limit_bytes=VMEM_LIMIT
         ),
         name="step",
-    )(flow_state, x_codes, y_codes)
+    )(flow_state, jnp.concatenate([x_codes, y_codes], axis=1))
     result = jnp.transpose(result.reshape(5, 8, 8, 128), (0, 2, 1, 3))
     return result.reshape(flow_state.shape)
 

time: 38.6 us -> 37.6 us (0.974)
  local copies, waits for them, and re-layouts: 1.59 us -> 0.67 us
  Pallas kernels: 36.8 us -> 36 us
  other arithmetic: 0 us -> 0.77 us
    unnamed x1, local copies, waits for them, and re-layouts: 1.59 us -> 0.67 us
    pallas_call x1, Pallas kernels: 36.8 us -> 36 us  [local(): pl.pallas_call(kernel, out_shape=jax.ShapeDtypeStruct((5, 64, 128), f32),...]
    concatenate x0 -> x1, other arithmetic: none -> 0.77 us  [local(): jnp.concatenate([x_codes, y_codes], axis=1)]
where the time goes in v4:
time: 37.6 us; the launch traced here: 37.5 us
  Pallas kernels  36 us (96%)
  other arithmetic  0.77 us (2%)
  local copies, waits for them, and re-layouts  0.67 us (2%)
    pallas_call x1, Pallas kernels, local(): pl.pallas_call(kernel, out_shape=jax.ShapeDtypeStruct((5, 64, 128), f32),...  36 us
    concatenate x1, other arithmetic, local(): jnp.concatenate([x_codes, y_codes], axis=1)  0.77 us

profile of v4, /device:TPU:1, one launch (start us, length us, event | category | flops | bytes accessed | tf_op | source)
XLA Modules:
  0.0 37.5 jit_solution(14595924070933885608)
XLA Ops:
  0.0 0.8 %pad_add_fusion.codes = s32[2,40]{1,0:T(2,128)S(1)} fusion(s32[2,8]{1,0:T(2,128)} %param.5, s32[2,32]{1,0:T(2,128)} %param.4), kind=kLoop, calls=%fused_computation | loop fusion | flops 80 | bytes 640 | tf_op jit(solution)/shard_map/concatenate | solution.py:714
  0.8 36.0 %step.1 = f32[5,64,128]{2,1,0:T(8,128)S(1)} custom-call(f32[5,8,1024]{2,1,0:T(8,128)} %flow.1, s32[2,40]{1,0:T(2,128)S(1)} %pad_add_fusion.codes), custom_call_target="tpu_custom_call" | custom-call | tf_op jit(solution)/shard_map/step/pallas_call | solution.py:671
  36.8 0.7 %copy.5 = f32[5,8,1024]{2,1,0:T(8,128)} copy(f32[5,8,1024]{2,1,0:T(8,128)S(1)} %bitcast.5) | data formatting | bytes 327680

commit v5 on v4

--- a/solution.py
+++ b/solution.py
@@ -10,7 +10,7 @@
 NZ = 32
 SX = 32
 SY = 16
-VMEM_LIMIT = 54950 * 1024
+VMEM_LIMIT = 32 * 1024 * 1024
 MAIN = 801.0
 GROUPS = ((0, (0,)), (2, (4,)), (1, (1, 2)), (1, (3,)))
 MESH = pl.DeviceIdType.MESH
@@ -362,7 +362,8 @@
 
 def kernel(
     flow,
-    codes,
+    x_codes,
+    y_codes,
     out,
     q_sc,
     part_sc,
@@ -388,7 +389,8 @@
     yb_out,
     yf_in,
     ys_sc,
-    code_sc,
+    x_code_sc,
+    y_code_sc,
     word,
     in_sem,
     code_sem,
@@ -422,8 +424,12 @@
         pltpu.make_async_copy(
             flow.at[:, :, pl.ds(128 * b, 128)], q_sc.at[:, pl.ds(8 * b, 8), :], in_sem
         ).start()
-    code_copy = pltpu.make_async_copy(codes, code_sc, code_sem)
-    code_copy.start()
+    code_copies = [
+        pltpu.make_async_copy(x_codes, x_code_sc, code_sem.at[0]),
+        pltpu.make_async_copy(y_codes, y_code_sc, code_sem.at[1]),
+    ]
+    for copy in code_copies:
+        copy.start()
 
     def tell(step):
         for k in (step + 1, 7 - step):
@@ -436,7 +442,8 @@
     pl.semaphore_wait(barrier, len(near))
     tell(0)
     wait_all(q_sc, in_sem)
-    code_copy.wait()
+    for copy in code_copies:
+        copy.wait()
 
     x_send[0] = q_sc[:, pl.ds(7, 8, stride=8), :]
     x_send[1] = q_sc[:, pl.ds(0, 8, stride=8), :]
@@ -497,7 +504,7 @@
         jnp.concatenate([prim_low[i][None], prim[i], prim_high[i][None]]) for i in (1, 6)
     )
 
-    lower, upper, first, last = x_bands(u, c, code_sc[:, 0:32], start_x, end_x)
+    lower, upper, first, last = x_bands(u, c, x_code_sc[...], start_x, end_x)
     xm, xg, xp, xq, x_own = eliminate(lower, upper, first, last)
     for group, (matrix, families) in enumerate(GROUPS):
         for row in range(4):
@@ -535,7 +542,7 @@
     speed_sc[...] = jnp.concatenate([down_y(speeds_y), up_y(speeds_y)]).reshape(4, 64, 128)
     speeds = jnp.stack([speed_sc[:, pl.ds(k, 8, stride=8), :] for k in range(8)], axis=1)
     y_lower, y_upper = y_bands(swap_groups(speeds))
-    y_lower, y_upper, first, last = y_ends(y_lower, y_upper, code_sc[:, 32:40], start_y, end_y)
+    y_lower, y_upper, first, last = y_ends(y_lower, y_upper, y_code_sc[...], start_y, end_y)
     ym, yg, yp, yq, y_own = eliminate(y_lower, y_upper, first, last)
     y_den, y_high_part, y_lev, y_p, y_q, y_joint, joined = y_join(y_own)
     ym_out[...] = jnp.zeros((32, 128), jnp.float32)
@@ -671,7 +678,7 @@
     result = pl.pallas_call(
         kernel,
         out_shape=jax.ShapeDtypeStruct((5, 64, 128), f32),
-        in_specs=[pl.BlockSpec(memory_space=pl.ANY)] * 2,
+        in_specs=[pl.BlockSpec(memory_space=pltpu.HBM)] * 3,
         out_specs=pl.BlockSpec(memory_space=pltpu.VMEM),
         scratch_shapes=[
             vmem(5, 64, 128),
@@ -698,10 +705,11 @@
             vmem(2, 16, 128),
             vmem(8, 16, 128),
             vmem(2, 16, 128),
-            pltpu.VMEM((2, 40), jnp.int32),
+            pltpu.VMEM((2, 32), jnp.int32),
+            pltpu.VMEM((2, 8), jnp.int32),
             pltpu.SemaphoreType.REGULAR((2,)),
             pltpu.SemaphoreType.DMA,
-            pltpu.SemaphoreType.DMA,
+            pltpu.SemaphoreType.DMA((2,)),
             pltpu.SemaphoreType.DMA((4,)),
             pltpu.SemaphoreType.DMA((4,)),
             pltpu.SemaphoreType.DMA((6,)),
@@ -711,7 +719,7 @@
             collective_id=0, has_side_effects=True, vmem_limit_bytes=VMEM_LIMIT
         ),
         name="step",
-    )(flow_state, jnp.concatenate([x_codes, y_codes], axis=1))
+    )(*(pltpu.with_memory_space_constraint(v, pltpu.HBM) for v in (flow_state, x_codes, y_codes)))
     result = jnp.transpose(result.reshape(5, 8, 8, 128), (0, 2, 1, 3))
     return result.reshape(flow_state.shape)
 

time: 37.6 us -> 36.8 us (0.979)
  other arithmetic: 0.77 us -> 0 us
    concatenate x1 -> x0, other arithmetic: 0.77 us -> none  [local(): jnp.concatenate([x_codes, y_codes], axis=1)]
where the time goes in v5:
time: 36.8 us; the launch traced here: 36.7 us
  Pallas kernels  36 us (98%)
  local copies, waits for them, and re-layouts  0.67 us (2%)
    pallas_call x1, Pallas kernels, local(): pl.pallas_call(kernel, out_shape=jax.ShapeDtypeStruct((5, 64, 128), f32),...  36 us

profile of v5, /device:TPU:1, one launch (start us, length us, event | category | flops | bytes accessed | tf_op | source)
XLA Modules:
  0.0 36.7 jit_solution(12572892180894807102)
XLA Ops:
  0.0 36.0 %step.1 = f32[5,64,128]{2,1,0:T(8,128)S(1)} custom-call(f32[5,8,1024]{2,1,0:T(8,128)} %flow.1, s32[2,32]{1,0:T(2,128)} %x_codes.1, s32[2,8]{1,0:T(2,128)} %y_codes.1), custom_call_target="tpu_custom_call" | custom-call | tf_op jit(solution)/shard_map/step/pallas_call | solution.py:678
  36.0 0.7 %copy.5 = f32[5,8,1024]{2,1,0:T(8,128)} copy(f32[5,8,1024]{2,1,0:T(8,128)S(1)} %bitcast.5) | data formatting | bytes 327680

commit v6 on v5

--- a/solution.py
+++ b/solution.py
@@ -468,20 +468,49 @@
     heard(0)
     tell(1)
 
+    two_families = lax.div(gx, 8) == 2
+
+    def by_rows(two, act):
+        @pl.when(two)
+        def _():
+            act(4)
+
+        @pl.when(jnp.logical_not(two))
+        def _():
+            act(2)
+
     def send_x(source, target, slot):
-        mine = pl.ds(gx * 4, 4)
-        pltpu.make_async_copy(source.at[mine], target.at[mine], recv_sem.at[slot]).start()
-
-        for dy, dx in X_ORDER:
-            other = 4 * lax.rem(lax.div(gx, 4) + dy, 8) + lax.rem(lax.rem(gx, 4) + dx, 4)
+        def own(rows):
+            mine = pl.ds(gx * 4, rows)
+            pltpu.make_async_copy(source.at[mine], target.at[mine], recv_sem.at[slot]).start()
+
+        def one(other, rows):
             pltpu.make_async_remote_copy(
-                src_ref=source.at[pl.ds(other * 4, 4)],
-                dst_ref=target.at[mine],
+                src_ref=source.at[pl.ds(other * 4, rows)],
+                dst_ref=target.at[pl.ds(gx * 4, rows)],
                 send_sem=send_sem.at[slot],
                 recv_sem=recv_sem.at[slot],
                 device_id=(other, gy),
                 device_id_type=MESH,
             ).start()
+
+        others = [x_at(dy, dx)[0] for dy, dx in X_ORDER]
+        if slot == 0:
+            own(4)
+            for other in others:
+                one(other, 4)
+        elif slot == 1:
+            by_rows(two_families, own)
+            for other in others:
+                by_rows(lax.div(other, 8) == 2, functools.partial(one, other))
+        else:
+
+            def all_of(rows):
+                own(rows)
+                for other in others:
+                    one(other, rows)
+
+            by_rows(two_families, all_of)
 
     def others_y():
         for dz, dc in Y_ORDER:
@@ -566,7 +595,7 @@
     wait_all(xm_in, recv_sem.at[0])
     den, high_part, a, c = factor([xm_in[pl.ds(row, SX, stride=4), :] for row in range(4)])
     levels = factor_levels(a, c)
-    wait_all(xr_in, recv_sem.at[1])
+    by_rows(two_families, lambda rows: wait_all(xr_in.at[pl.ds(0, SX * rows)], recv_sem.at[1]))
     for i in range(2):
         own_last = xr_in[pl.ds(2 * i, SX, stride=4), :]
         own_first = xr_in[pl.ds(2 * i + 1, SX, stride=4), :]
@@ -592,7 +621,7 @@
     half_rc_inv = 0.5 / rc
     c2_inv = 1.0 / prim[5]
 
-    wait_all(xs_in, recv_sem.at[2])
+    wait_all(xs_in.at[pl.ds(0, 80)], recv_sem.at[2])
 
     def x_value(kind):
         rows = []
@@ -662,8 +691,11 @@
 
     for copy in copies:
         copy.wait_send()
-    for slot in range(3):
-        wait_all(xm_out.at[pl.ds(0, 4 * (SX - 1))], send_sem.at[slot])
+    wait_all(xm_out.at[pl.ds(0, 4 * (SX - 1))], send_sem.at[0])
+    by_rows(two_families, lambda rows: wait_all(xr_out.at[pl.ds(0, 80 - rows)], send_sem.at[1]))
+    by_rows(
+        two_families, lambda rows: wait_all(xs_out.at[pl.ds(0, (SX - 1) * rows)], send_sem.at[2])
+    )
     wait_all(ym_in.at[pl.ds(0, SY - 1)], send_sem.at[3])
     wait_all(yf_in.at[pl.ds(0, 7), pl.ds(0, 10)], send_sem.at[4])
     core_copy.wait_send()

time: 36.8 us -> 36.8 us (level)
  no operation moved by 1% of the time
where the time goes in v6:
time: 36.8 us; the launch traced here: 36.7 us
  Pallas kernels  36 us (98%)
  local copies, waits for them, and re-layouts  0.67 us (2%)
    pallas_call x1, Pallas kernels, local(): pl.pallas_call(kernel, out_shape=jax.ShapeDtypeStruct((5, 64, 128), f32),...  36 us

profile of v6, /device:TPU:1, one launch (start us, length us, event | category | flops | bytes accessed | tf_op | source)
XLA Modules:
  0.0 36.7 jit_solution(7971402998976845887)
XLA Ops:
  0.0 36.0 %step.1 = f32[5,64,128]{2,1,0:T(8,128)S(1)} custom-call(f32[5,8,1024]{2,1,0:T(8,128)} %flow.1, s32[2,32]{1,0:T(2,128)} %x_codes.1, s32[2,8]{1,0:T(2,128)} %y_codes.1), custom_call_target="tpu_custom_call" | custom-call | tf_op jit(solution)/shard_map/step/pallas_call | solution.py:710
  36.0 0.7 %copy.5 = f32[5,8,1024]{2,1,0:T(8,128)} copy(f32[5,8,1024]{2,1,0:T(8,128)S(1)} %bitcast.5) | data formatting | bytes 327680

commit v7 on v6

--- a/solution.py
+++ b/solution.py
@@ -533,14 +533,6 @@
         jnp.concatenate([prim_low[i][None], prim[i], prim_high[i][None]]) for i in (1, 6)
     )
 
-    lower, upper, first, last = x_bands(u, c, x_code_sc[...], start_x, end_x)
-    xm, xg, xp, xq, x_own = eliminate(lower, upper, first, last)
-    for group, (matrix, families) in enumerate(GROUPS):
-        for row in range(4):
-            xm_out[pl.ds(group * 32 + row, 8, stride=4), :] = x_own[row][matrix]
-    heard(1)
-    send_x(xm_out, xm_in, 0)
-
     y_edge_low = jnp.where(start_y, roll(blocks[:, 0], 96, -1), y_low[...])
     y_edge_high = jnp.where(end_y, roll(blocks[:, 7], 32, -1), y_high[...])
     low_terms = y_terms(y_edge_low, primitives(y_edge_low))
@@ -557,6 +549,15 @@
         + jnp.stack([part_sc[:, pl.ds(k, 8, stride=8), :] for k in range(8)], axis=1)
     )
     right = x_right(residual, prim)
+
+    lower, upper, first, last = x_bands(u, c, x_code_sc[...], start_x, end_x)
+    xm, xg, xp, xq, x_own = eliminate(lower, upper, first, last)
+    for group, (matrix, families) in enumerate(GROUPS):
+        for row in range(4):
+            xm_out[pl.ds(group * 32 + row, 8, stride=4), :] = x_own[row][matrix]
+    heard(1)
+    send_x(xm_out, xm_in, 0)
+
     xd, x_last = eliminate_right([right[:, k] for k in range(8)], lower, xm, xg)
     zero = jnp.zeros((8, 128), jnp.float32)
     for group, (matrix, families) in enumerate(GROUPS):

time: 36.8 us -> 36.8 us (level)
  no operation moved by 1% of the time
where the time goes in v7:
time: 36.8 us; the launch traced here: 36.7 us
  Pallas kernels  36 us (98%)
  local copies, waits for them, and re-layouts  0.67 us (2%)
    pallas_call x1, Pallas kernels, local(): pl.pallas_call(kernel, out_shape=jax.ShapeDtypeStruct((5, 64, 128), f32),...  36 us

profile of v7, /device:TPU:1, one launch (start us, length us, event | category | flops | bytes accessed | tf_op | source)
XLA Modules:
  0.0 36.7 jit_solution(6481344948313823489)
XLA Ops:
  0.0 36.0 %step.1 = f32[5,64,128]{2,1,0:T(8,128)S(1)} custom-call(f32[5,8,1024]{2,1,0:T(8,128)} %flow.1, s32[2,32]{1,0:T(2,128)} %x_codes.1, s32[2,8]{1,0:T(2,128)} %y_codes.1), custom_call_target="tpu_custom_call" | custom-call | tf_op jit(solution)/shard_map/step/pallas_call | solution.py:711
  36.0 0.7 %copy.5 = f32[5,8,1024]{2,1,0:T(8,128)} copy(f32[5,8,1024]{2,1,0:T(8,128)S(1)} %bitcast.5) | data formatting | bytes 327680

commit v8 on v7

--- a/solution.py
+++ b/solution.py
@@ -597,13 +597,17 @@
     den, high_part, a, c = factor([xm_in[pl.ds(row, SX, stride=4), :] for row in range(4)])
     levels = factor_levels(a, c)
     by_rows(two_families, lambda rows: wait_all(xr_in.at[pl.ds(0, SX * rows)], recv_sem.at[1]))
-    for i in range(2):
-        own_last = xr_in[pl.ds(2 * i, SX, stride=4), :]
-        own_first = xr_in[pl.ds(2 * i + 1, SX, stride=4), :]
-        d = den * own_last + high_part * roll(own_first, -1, 0)
-        d = reduce_levels(d, levels)
-        xs_out[pl.ds(2 * i, SX, stride=4), :] = roll(d, 1, 0)
-        xs_out[pl.ds(2 * i + 1, SX, stride=4), :] = d
+
+    def solve_x(rows):
+        for i in range(rows // 2):
+            own_last = xr_in[pl.ds(2 * i, SX, stride=4), :]
+            own_first = xr_in[pl.ds(2 * i + 1, SX, stride=4), :]
+            d = den * own_last + high_part * roll(own_first, -1, 0)
+            d = reduce_levels(d, levels)
+            xs_out[pl.ds(2 * i, SX, stride=4), :] = roll(d, 1, 0)
+            xs_out[pl.ds(2 * i + 1, SX, stride=4), :] = d
+
+    by_rows(two_families, solve_x)
     send_x(xs_out, xs_in, 2)
 
     wait_all(ym_in, recv_sem.at[3])

time: 36.8 us -> 36.8 us (level)
  no operation moved by 1% of the time
where the time goes in v8:
time: 36.8 us; the launch traced here: 36.7 us
  Pallas kernels  36 us (98%)
  local copies, waits for them, and re-layouts  0.67 us (2%)
    pallas_call x1, Pallas kernels, local(): pl.pallas_call(kernel, out_shape=jax.ShapeDtypeStruct((5, 64, 128), f32),...  36 us

profile of v8, /device:TPU:1, one launch (start us, length us, event | category | flops | bytes accessed | tf_op | source)
XLA Modules:
  0.0 36.7 jit_solution(13350818692578580472)
XLA Ops:
  0.0 36.0 %step.1 = f32[5,64,128]{2,1,0:T(8,128)S(1)} custom-call(f32[5,8,1024]{2,1,0:T(8,128)} %flow.1, s32[2,32]{1,0:T(2,128)} %x_codes.1, s32[2,8]{1,0:T(2,128)} %y_codes.1), custom_call_target="tpu_custom_call" | custom-call | tf_op jit(solution)/shard_map/step/pallas_call | solution.py:715
  36.0 0.7 %copy.5 = f32[5,8,1024]{2,1,0:T(8,128)} copy(f32[5,8,1024]{2,1,0:T(8,128)S(1)} %bitcast.5) | data formatting | bytes 327680
